TPU v7x, 32 devices: a whole 2x2x4 slice. The times are simulated.
32 devices in a mesh: feat: 8 (over y, x, core), node: 4 (over z).
Axes of the slice: x: 2, y: 2, z: 4, core: 2. Of those that a mesh axis runs over, the one named last changes fastest.
Arguments:
- features: bfloat16 [4, 512, 16384], P('node', 'feat'), may hold values from -6 to 6
- target_ids: int32 [4, 4096], P('node'), may hold values from 0 to 16383
- block_ids: int32 [4, 32, 8], P('node'), may hold values from 0 to 127
- tile_counts: int32 [4, 32], P('node'), may hold values from 1 to 8, as said below
- adjacency: bfloat16 [4, 32, 8, 128, 128], P('node'), may hold values from 0 to 0.25
- w_neigh: bfloat16 [256, 512], P(None, 'feat'), may hold values from -0.1875 to 0.1875
- w_self: bfloat16 [256, 512], P(None, 'feat'), may hold values from -0.1875 to 0.1875
- w_head: bfloat16 [256, 256], replicated, may hold values from -0.375 to 0.375
- grad_scores: bfloat16 [4, 4096, 256], P('node', 'feat'), may hold values from -6 to 6
Outputs:
- scores: bfloat16 [4, 4096, 256], P('node', 'feat')
- grad_head: float32 [256, 256], replicated
- grad_neigh: float32 [256, 512], P(None, 'feat')
- grad_self: float32 [256, 512], P(None, 'feat')
Inputs may be any that keep to these rules, and one draw needn't show every extreme that they name: `tile_counts`: one group, drawn from the seed, has all of its tiles at 8 live slots; every tile of the other groups has fewer than 8.
All inputs are finite; a program needn't handle non-finite values.
Results may differ from a plain program's by a relative error of at most 0.0056.
Values may be sent and summed in bfloat16 or wider, within the bound.
A program may use at most 64 MiB of HBM per device.

v0:
```python
import jax
import jax.numpy as jnp
from jax import lax
from jax.sharding import PartitionSpec as P


def aggregate_local(feature_rows, block_row, count_row, adjacency_group):
    width = feature_rows.shape[0]
    tiles = block_row.shape[0]
    slots = block_row.shape[1]
    blocks = feature_rows.reshape(width, -1, 128)
    gathered = jnp.take(blocks, block_row.reshape(-1), axis=1).reshape(width, tiles, slots, 128)
    live = (jnp.arange(slots, dtype=jnp.int32)[None, :] < count_row[:, None]).astype(jnp.bfloat16)
    masked = gathered * live[None, :, :, None]
    summed = jnp.einsum(
        "tkrs,ftks->ftr", adjacency_group, masked, preferred_element_type=jnp.float32
    )
    summed = summed / count_row.astype(jnp.float32)[None, :, None]
    return summed.astype(jnp.bfloat16).reshape(width, tiles * 128)


def contract_first(left, right):
    return lax.dot_general(
        left, right, (((0,), (1,)), ((), ())), preferred_element_type=jnp.float32
    )


def body(
    features, target_ids, block_ids, tile_counts, adjacency, w_neigh, w_self, w_head, grad_scores
):
    feature_rows = features[0]
    aggregate = aggregate_local(feature_rows, block_ids[0], tile_counts[0], adjacency[0])
    own = jnp.take(feature_rows, target_ids[0], axis=1)
    agg_part = aggregate
    own_part = own
    preact = lax.psum_scatter(
        contract_first(agg_part, w_neigh) + contract_first(own_part, w_self),
        "feat",
        scatter_dimension=0,
        tiled=True,
    )
    hidden = jax.nn.silu(preact).astype(jnp.bfloat16)
    scores = jnp.dot(hidden, w_head.T, preferred_element_type=jnp.float32).astype(jnp.bfloat16)
    cotangent = grad_scores[0]
    head_local = lax.dot_general(
        cotangent, hidden, (((0,), (0,)), ((), ())), preferred_element_type=jnp.float32
    )
    grad_head = lax.psum(head_local, ("feat", "node"))
    grad_hidden = jnp.dot(cotangent, w_head, preferred_element_type=jnp.float32)
    sigma = jax.nn.sigmoid(preact)
    grad_pre = (grad_hidden * sigma * (1.0 + preact * (1.0 - sigma))).astype(jnp.bfloat16)
    shard_piece = lax.all_gather(grad_pre, "feat", axis=0, tiled=True)
    agg_part = aggregate
    own_part = own
    neigh_local = contract_first(shard_piece, agg_part)
    self_local = contract_first(shard_piece, own_part)
    grad_neigh, grad_self = lax.psum((neigh_local, self_local), "node")
    return (scores[None], grad_head, grad_neigh, grad_self)


def solution(mesh):
    in_specs = (
        P("node", "feat", None),
        P("node", None),
        P("node", None, None),
        P("node", None),
        P("node", None, None, None, None),
        P(None, "feat"),
        P(None, "feat"),
        P(),
        P("node", "feat", None),
    )
    out_specs = (P("node", "feat", None), P(), P(None, "feat"), P(None, "feat"))
    return jax.shard_map(body, mesh=mesh, in_specs=in_specs, out_specs=out_specs, check_vma=False)
```

profile of v0, /device:TPU:0, one launch (start us, length us, event | category | flops | bytes accessed | tf_op | source)
XLA Modules:
  0.0 308.8 jit_solution(13335983999297234126)
XLA Ops:
  7.2 0.8 compare_and_fusion.1
  8.1 0.8 copy.23
  9.6 0.7 compare_select_fusion
  10.3 0.7 compare_and_fusion
  11.1 0.7 fusion.33
  11.9 4.8 %copy.26 = bf16[1,64,16384]{1,2,0:T(8,128)(2,1)} copy(bf16[1,64,16384]{2,1,0:T(8,128)(2,1)} %param.9) | data formatting | bytes 4194304 | tf_op args[0]
  17.3 1.4 copy.24
  18.6 3.1 gather_fusion
  21.7 13.8 %gather_fusion.1 = bf16[4096,64]{1,0:T(8,128)(2,1)S(1)} fusion(bf16[64,16384]{0,1:T(8,128)(2,1)} %bitcast.57, s32[4096]{0:T(1024)S(1)} %broadcast_clamp_fusion), kind=kCustom, calls=%fused_computation.1 | custom fusion | bytes 1064960 | tf_op jit(solution)/shard_map/jit(_take)/gather | solution.py:33
  35.5 1.5 fusion.29
  37.7 5.7 %fusion.19 = bf16[32,8,8,128]{3,2,1,0:T(8,128)(2,1)S(1)} fusion(bf16[1,32,8,128,128]{4,3,2,1,0:T(8,128)(2,1)} %param.13, bf16[64,32,8,128]{3,0,2,1:T(8,128)(2,1)S(1)} %bitcast.60, pred[32,8]{1,0:T(8,128)(4,1)S(1)} %copy.22, bf16[32,8]{1,0:T(8,128)(2,1)S(1)} %fusion.33, f32[32]{0:T(128)S(1)} %bitcast_convert_fusion), kind=kOutput, calls=%fused_computation.19 | convolution fusion | flops 541589504 | bytes 13108096 | tf_op jit(solution)/shard_map/tkrs,ftks->ftr/dot_general | solution.py:15
  43.4 2.7 convolution_add_fusion
  46.2 54.1 %reduce-scatter.2.cloned.1.call-done = f32[512,256]{1,0:T(8,128)} async-done(((f32[4096,256]{1,0:T(8,128)}), f32[512,256]{1,0:T(8,128)}) %reduce-scatter.2.cloned.1.call-update) | async-done | bytes 524304 | tf_op jit(solution)/shard_map/reduce_scatter | solution.py:36
  100.3 2.0 fusion.13
  102.4 2.1 convolution_bitcast_fusion
  104.6 26.3 %all-gather.2.cloned.1.call-done = bf16[4096,256]{1,0:T(8,128)(2,1)} async-done(((bf16[512,256]{1,0:T(8,128)(2,1)}), bf16[4096,256]{1,0:T(8,128)(2,1)}) %all-gather.2.cloned.1.call-update) | async-done | bytes 2097168 | tf_op jit(solution)/shard_map/all_gather | solution.py:52
  130.9 4.9 %fusion.30 = f32[256,64]{0,1:T(8,128)} fusion(bf16[4096,256]{1,0:T(8,128)(2,1)} %all-gather.2.cloned.1.call-done, bf16[4096,64]{1,0:T(8,128)(2,1)S(1)} %gather_fusion.1, pred[4096]{0:T(1024)(128)(4,1)S(1)} %compare_and_fusion), kind=kOutput, calls=%fused_computation.28 | convolution fusion | flops 134479872 | bytes 2691072 | tf_op jit(solution)/shard_map/dot_general | solution.py:23
  135.8 1.1 fusion.24
  136.9 1.0 fusion.14
  137.9 124.9 %all-reduce.4.cloned.1.call-done = f32[256,256]{0,1:T(8,128)} async-done(((f32[256,256]{0,1:T(8,128)}), f32[256,256]{0,1:T(8,128)}) %all-reduce.4.cloned.1.call-update) | async-done | bytes 262160 | tf_op jit(solution)/shard_map/psum | solution.py:48
  262.9 1.8 copy.27
  264.6 34.7 %all-reduce.6.cloned.1.call-done = (f32[256,64]{0,1:T(8,128)}, f32[256,64]{0,1:T(8,128)}) async-done(((f32[256,64]{0,1:T(8,128)}, f32[256,64]{0,1:T(8,128)}), (f32[256,64]{0,1:T(8,128)}, f32[256,64]{0,1:T(8,128)})) %all-reduce.6.cloned.1.call-update) | async-done | bytes 131088 | tf_op jit(solution)/shard_map/psum | solution.py:57
  299.4 1.5 copy.42
  300.8 1.5 copy.43
  (31 shorter events, 2.4 us)
Async XLA Ops:
  7.2 93.1 %copy-start = (bf16[1,512,256]{2,1,0:T(8,128)(2,1)S(1)}, bf16[1,512,256]{2,1,0:T(8,128)(2,1)}, u32[]{:S(2)}) copy-start(bf16[1,512,256]{2,1,0:T(8,128)(2,1)} %param.17) | copy-start | bytes 786436
  7.2 9.5 %copy-start.1 = (bf16[1,64,16384]{2,1,0:T(8,128)(2,1)S(1)}, bf16[1,64,16384]{2,1,0:T(8,128)(2,1)}, u32[]{:S(2)}) copy-start(bf16[1,64,16384]{2,1,0:T(8,128)(2,1)} %param.9) | copy-start | bytes 6291460
  7.2 93.1 %reduce-scatter.2.cloned.1.call-start = ((), (), s32[]{:S(2)}) async-start(), calls=%async_computation.1 | async-start | bytes 4718592 | tf_op jit(solution)/shard_map/reduce_scatter | solution.py:36
  21.7 13.8 %copy-start.4 = (bf16[256,64]{0,1:T(8,128)(2,1)S(1)}, bf16[256,64]{0,1:T(8,128)(2,1)}, u32[]{:S(2)}) copy-start(bf16[256,64]{0,1:T(8,128)(2,1)} %param.15) | copy-start | bytes 98308
  35.5 2.2 copy-start.2
  37.7 5.7 %copy-start.5 = (bf16[256,64]{0,1:T(8,128)(2,1)S(1)}, bf16[256,64]{0,1:T(8,128)(2,1)}, u32[]{:S(2)}) copy-start(bf16[256,64]{0,1:T(8,128)(2,1)} %param.14) | copy-start | bytes 98308
  46.1 54.2 %copy-start.7 = (bf16[256,256]{1,0:T(8,128)(2,1)S(1)}, bf16[256,256]{1,0:T(8,128)(2,1)}, u32[]{:S(2)}) copy-start(bf16[256,256]{1,0:T(8,128)(2,1)} %param.16) | copy-start | bytes 393220
  46.1 84.7 %all-gather.2.cloned.1.call-start = ((), (), s32[]{:S(2)}) async-start(), calls=%async_computation.3 | async-start | bytes 2359296 | tf_op jit(solution)/shard_map/all_gather | solution.py:52
  102.4 160.5 %all-reduce.4.cloned.1.call-start = ((), (), s32[]{:S(2)}) async-start(), calls=%async_computation.2 | async-start | bytes 524288 | tf_op jit(solution)/shard_map/psum | solution.py:48
  104.5 32.5 %copy-start.6 = (f32[512,256]{1,0:T(8,128)S(1)}, f32[512,256]{1,0:T(8,128)}, u32[]{:S(2)}) copy-start(f32[512,256]{1,0:T(8,128)} %reduce-scatter.2.cloned.1.call-done) | copy-start | bytes 1572868
  104.5 194.9 %all-reduce.6.cloned.1.call-start = ((), (), s32[]{:S(2)}) async-start(), calls=%async_computation.4 | async-start | bytes 262144 | tf_op jit(solution)/shard_map/psum | solution.py:57
  130.8 4.9 %copy-start.3 = (bf16[4096,256]{1,0:T(8,128)(2,1)S(1)}, bf16[4096,256]{1,0:T(8,128)(2,1)}, u32[]{:S(2)}) copy-start(bf16[4096,256]{1,0:T(8,128)(2,1)} %all-gather.2.cloned.1.call-done) | copy-start | bytes 6291460
Sparse Core Ops, SparseCore 0:
  46.2 53.9 reduce-scatter.1
  102.9 27.8 all-gather.1
  137.8 124.9 all-reduce.3
  265.8 33.5 all-reduce.5
where the time goes:
time: 309 us
  waiting for transfers between devices  240 us (78%)
  local copies, waits for them, and re-layouts  30 us (10%)
  matrix products  21 us (7%)
  between operations  13.9 us (4%)
  other arithmetic  3.71 us (1%)
    psum x1, waiting for transfers between devices, body(): grad_head = lax.psum(head_local, ('feat', 'node'))  125 us
    reduce_scatter x1, waiting for transfers between devices, body(): lax.psum_scatter(contract_first(agg_part, w_neigh) + contract_first(own_p...  54.1 us
    psum x1, waiting for transfers between devices, body(): grad_neigh, grad_self = lax.psum((neigh_local, self_local), 'node')  34.7 us
    all_gather x1, waiting for transfers between devices, body(): shard_piece = lax.all_gather(grad_pre, 'feat', axis=0, tiled=True)  26.3 us
    gather x1, local copies, waits for them, and re-layouts, body(): own = jnp.take(feature_rows, target_ids[0], axis=1)  13.8 us
    unnamed x22, local copies, waits for them, and re-layouts  11.6 us
    dot_general x4, matrix products, contract_first(): lax.dot_general(left, right, (((0,), (1,)), ((), ())), preferred_element_...  10.2 us
  transfers between devices with their start and end apart: 4, of which 4 were waited for; matrix products, arithmetic and copies ran while one was open for 4% of the time, Pallas kernels for 0%

commit v1 on v0

--- a/solution.py
+++ b/solution.py
@@ -49,7 +49,15 @@
     grad_hidden = jnp.dot(cotangent, w_head, preferred_element_type=jnp.float32)
     sigma = jax.nn.sigmoid(preact)
     grad_pre = (grad_hidden * sigma * (1.0 + preact * (1.0 - sigma))).astype(jnp.bfloat16)
-    shard_piece = lax.all_gather(grad_pre, "feat", axis=0, tiled=True)
+    ways, here, turn = (lax.axis_size("feat"), lax.axis_index("feat"), grad_pre.shape[0])
+    line, have = (grad_pre, 1)
+    while have < ways:
+        line = jnp.concatenate(
+            [line, lax.ppermute(line, "feat", [(d, (d - have) % ways) for d in range(ways)])],
+            axis=0,
+        )
+        have = 2 * have
+    shard_piece = jnp.roll(line, here * turn, axis=0)
     agg_part = aggregate
     own_part = own
     neigh_local = contract_first(shard_piece, agg_part)

time: 309 us -> 296 us (0.958)
  waiting for transfers between devices: 240 us -> 216 us
  local copies, waits for them, and re-layouts: 30 us -> 36.9 us
  starting transfers between devices: 0.16 us -> 4.17 us
    ppermute x0 -> x3, waiting for transfers between devices: none -> 37.5 us  [body(): lax.ppermute(line, 'feat', [(d, (d - have) % ways) for d in range(ways)])]
    psum x1, waiting for transfers between devices: 125 us -> 89.4 us  [body(): grad_head = lax.psum(head_local, ('feat', 'node'))]
    all_gather x1 -> x0, waiting for transfers between devices: 26.3 us -> none  [body(): shard_piece = lax.all_gather(grad_pre, 'feat', axis=0, tiled=True)]
    unnamed x22 -> x36, local copies, waits for them, and re-layouts: 11.6 us -> 17.5 us
    ppermute x0 -> x3, starting transfers between devices: none -> 4.05 us  [body(): lax.ppermute(line, 'feat', [(d, (d - have) % ways) for d in range(ways)])]
  transfers between devices with their start and end apart: 4 -> 6, of which waited for: 4 -> 6; matrix products, arithmetic and copies ran while one was open for 4% -> 6% of each run, Pallas kernels for 0% -> 0%
where the time goes in v1:
time: 296 us; the launch traced here: 295 us
  waiting for transfers between devices  216 us (73%)
  local copies, waits for them, and re-layouts  36.9 us (12%)
  matrix products  22.4 us (8%)
  between operations  13.9 us (5%)
  starting transfers between devices  4.17 us (1%)
    psum x1, waiting for transfers between devices, body(): grad_head = lax.psum(head_local, ('feat', 'node'))  89.4 us
    reduce_scatter x1, waiting for transfers between devices, body(): lax.psum_scatter(contract_first(agg_part, w_neigh) + contract_first(own_p...  54.1 us
    ppermute x3, waiting for transfers between devices, body(): lax.ppermute(line, 'feat', [(d, (d - have) % ways) for d in range(ways)])  37.5 us
    psum x1, waiting for transfers between devices, body(): grad_neigh, grad_self = lax.psum((neigh_local, self_local), 'node')  34.9 us
    unnamed x36, local copies, waits for them, and re-layouts  17.5 us
    gather x1, local copies, waits for them, and re-layouts, body(): own = jnp.take(feature_rows, target_ids[0], axis=1)  13.8 us
    dot_general x4, matrix products, contract_first(): lax.dot_general(left, right, (((0,), (1,)), ((), ())), preferred_element_...  11.7 us
  transfers between devices with their start and end apart: 6, of which 6 were waited for; matrix products, arithmetic and copies ran while one was open for 6% of the time, Pallas kernels for 0%

profile of v1, /device:TPU:0, one launch (start us, length us, event | category | flops | bytes accessed | tf_op | source)
XLA Modules:
  0.0 295.2 jit_solution(17359947115163122103)
XLA Ops:
  8.9 4.8 %copy.26 = bf16[1,64,16384]{1,2,0:T(8,128)(2,1)} copy(bf16[1,64,16384]{2,1,0:T(8,128)(2,1)} %param.9) | data formatting | bytes 4194304 | tf_op args[0]
  14.3 1.4 copy.24
  16.0 13.8 %gather_fusion.1 = bf16[4096,64]{1,0:T(8,128)(2,1)S(1)} fusion(bf16[64,16384]{0,1:T(8,128)(2,1)} %bitcast.57, s32[4096]{0:T(1024)S(1)} %broadcast_clamp_fusion), kind=kCustom, calls=%fused_computation.1 | custom fusion | bytes 1064960 | tf_op jit(solution)/shard_map/jit(_take)/gather | solution.py:33
  29.7 3.1 %gather_fusion = bf16[256,64,128]{2,1,0:T(8,128)(2,1)} fusion(bf16[64,128,128]{2,0,1:T(8,128)(2,1)S(1)} %copy.24, s32[1024]{0:T(1024)S(1)} %pad_clamp_fusion), kind=kCustom, calls=%fused_computation | custom fusion | bytes 8389632 | tf_op jit(solution)/shard_map/jit(_take)/gather | solution.py:12
  32.8 1.4 fusion.32
  35.0 5.6 %fusion.23 = bf16[32,8,8,128]{3,2,1,0:T(8,128)(2,1)S(1)} fusion(bf16[1,32,8,128,128]{4,3,2,1,0:T(8,128)(2,1)} %param.13, bf16[64,32,8,128]{3,0,2,1:T(8,128)(2,1)S(1)} %bitcast.60, pred[32,8]{1,0:T(8,128)(4,1)S(1)} %copy.22, bf16[32,8]{1,0:T(8,128)(2,1)S(1)} %fusion.35, f32[32]{0:T(128)S(1)} %bitcast_convert_fusion), kind=kOutput, calls=%fused_computation.24 | convolution fusion | flops 541589504 | bytes 13108096 | tf_op jit(solution)/shard_map/tkrs,ftks->ftr/dot_general | solution.py:15
  41.4 2.7 convolution_add_fusion
  44.2 54.1 %reduce-scatter.2.cloned.1.call-done = f32[512,256]{1,0:T(8,128)} async-done(((f32[4096,256]{1,0:T(8,128)}), f32[512,256]{1,0:T(8,128)}) %reduce-scatter.2.cloned.1.call-update) | async-done | bytes 524304 | tf_op jit(solution)/shard_map/reduce_scatter | solution.py:36
  98.3 2.0 constant_dynamic-update-slice_fusion.7
  101.3 3.9 %collective-permute-done = bf16[512,256]{1,0:T(8,128)(2,1)S(1)} collective-permute-done((bf16[512,256]{1,0:T(8,128)(2,1)S(1)}, bf16[512,256]{1,0:T(8,128)(2,1)S(1)}, u32[]{:S(2)}, u32[]{:S(2)}) %collective-permute-start) | collective-permute-done | bytes 262176 | tf_op jit(solution)/shard_map/ppermute | solution.py:56
  105.2 1.5 collective-permute-start.1
  106.7 13.0 %collective-permute-done.1 = bf16[1024,256]{1,0:T(8,128)(2,1)S(1)} collective-permute-done((bf16[1024,256]{1,0:T(8,128)(2,1)S(1)}, bf16[1024,256]{1,0:T(8,128)(2,1)S(1)}, u32[]{:S(2)}, u32[]{:S(2)}) %collective-permute-start.1) | collective-permute-done | bytes 524320 | tf_op jit(solution)/shard_map/ppermute | solution.py:56
  120.7 1.7 collective-permute-start.2
  122.4 2.1 convolution_bitcast_fusion
  126.1 20.6 %collective-permute-done.2 = bf16[2048,256]{1,0:T(8,128)(2,1)S(1)} collective-permute-done((bf16[2048,256]{1,0:T(8,128)(2,1)}, bf16[2048,256]{1,0:T(8,128)(2,1)S(1)}, u32[]{:S(2)}, u32[]{:S(2)}) %collective-permute-start.2) | collective-permute-done | bytes 1048608 | tf_op jit(solution)/shard_map/ppermute | solution.py:56
  146.7 1.1 constant_dynamic-update-slice_fusion.4
  150.1 1.1 constant_dynamic-update-slice_fusion
  151.2 4.8 %fusion.7 = f32[256,64]{0,1:T(8,128)} fusion(bf16[8192,256]{1,0:T(8,128)(2,1)} %constant_dynamic-update-slice_fusion, s32[]{:T(128)S(6)} %select_n.62, bf16[4096,64]{1,0:T(8,128)(2,1)S(1)} %gather_fusion.1, pred[4096]{0:T(1024)(128)(4,1)S(1)} %compare_and_fusion), kind=kOutput, calls=%fused_computation.10 | convolution fusion | flops 134479872 | bytes 2691076 | tf_op jit(solution)/shard_map/dot_general | solution.py:23
  155.9 2.7 fusion.9
  159.7 89.4 %all-reduce.4.cloned.1.call-done = f32[256,256]{0,1:T(8,128)} async-done(((f32[256,256]{0,1:T(8,128)}), f32[256,256]{0,1:T(8,128)}) %all-reduce.4.cloned.1.call-update) | async-done | bytes 262160 | tf_op jit(solution)/shard_map/psum | solution.py:48
  249.1 1.8 copy.27
  250.9 34.9 %all-reduce.6.cloned.1.call-done = (f32[256,64]{0,1:T(8,128)}, f32[256,64]{0,1:T(8,128)}) async-done(((f32[256,64]{0,1:T(8,128)}, f32[256,64]{0,1:T(8,128)}), (f32[256,64]{0,1:T(8,128)}, f32[256,64]{0,1:T(8,128)})) %all-reduce.6.cloned.1.call-update) | async-done | bytes 131088 | tf_op jit(solution)/shard_map/psum | solution.py:65
  285.8 1.5 copy.49
  287.2 1.5 copy.50
  (51 shorter events, 11.0 us)
Async XLA Ops:
  7.2 91.2 %copy-start = (bf16[1,512,256]{2,1,0:T(8,128)(2,1)S(1)}, bf16[1,512,256]{2,1,0:T(8,128)(2,1)}, u32[]{:S(2)}) copy-start(bf16[1,512,256]{2,1,0:T(8,128)(2,1)} %param.17) | copy-start | bytes 786436
  7.2 6.5 %copy-start.1 = (bf16[1,64,16384]{2,1,0:T(8,128)(2,1)S(1)}, bf16[1,64,16384]{2,1,0:T(8,128)(2,1)}, u32[]{:S(2)}) copy-start(bf16[1,64,16384]{2,1,0:T(8,128)(2,1)} %param.9) | copy-start | bytes 6291460
  7.2 6.5 %copy-start.5 = (s32[1,4096]{1,0:T(1,128)S(1)}, s32[1,4096]{1,0:T(1,128)}, u32[]{:S(2)}) copy-start(s32[1,4096]{1,0:T(1,128)} %param.10) | copy-start | bytes 49156
  7.2 91.1 %reduce-scatter.2.cloned.1.call-start = ((), (), s32[]{:S(2)}) async-start(), calls=%async_computation.1 | async-start | bytes 4718592 | tf_op jit(solution)/shard_map/reduce_scatter | solution.py:36
  13.7 2.1 copy-start.8
  29.7 3.1 %copy-start.6 = (bf16[256,64]{0,1:T(8,128)(2,1)S(1)}, bf16[256,64]{0,1:T(8,128)(2,1)}, u32[]{:S(2)}) copy-start(bf16[256,64]{0,1:T(8,128)(2,1)} %param.15) | copy-start | bytes 98308
  32.8 2.2 copy-start.2
  35.0 6.5 %copy-start.7 = (bf16[256,64]{0,1:T(8,128)(2,1)S(1)}, bf16[256,64]{0,1:T(8,128)(2,1)}, u32[]{:S(2)}) copy-start(bf16[256,64]{0,1:T(8,128)(2,1)} %param.14) | copy-start | bytes 98308
  40.6 0.8 copy-start.3
  44.1 54.2 %copy-start.10 = (bf16[256,256]{1,0:T(8,128)(2,1)S(1)}, bf16[256,256]{1,0:T(8,128)(2,1)}, u32[]{:S(2)}) copy-start(bf16[256,256]{1,0:T(8,128)(2,1)} %param.16) | copy-start | bytes 393220
  44.2 204.9 %all-reduce.4.cloned.1.call-start = ((), (), s32[]{:S(2)}) async-start(), calls=%async_computation.2 | async-start | bytes 524288 | tf_op jit(solution)/shard_map/psum | solution.py:48
  100.4 4.8 %collective-permute-start = (bf16[512,256]{1,0:T(8,128)(2,1)S(1)}, bf16[512,256]{1,0:T(8,128)(2,1)S(1)}, u32[]{:S(2)}, u32[]{:S(2)}) collective-permute-start(bf16[512,256]{1,0:T(8,128)(2,1)S(1)} %get-tuple-element.19), channel_id=1, source_target_pairs={{0,28},{4,0},{8,4},{12,8},{16,12},{20,16},{24,20},{28,24},{1,29},{... | collective-permute-start | bytes 786440 | tf_op jit(solution)/shard_map/ppermute | solution.py:56
  105.2 14.5 %collective-permute-start.1 = (bf16[1024,256]{1,0:T(8,128)(2,1)S(1)}, bf16[1024,256]{1,0:T(8,128)(2,1)S(1)}, u32[]{:S(2)}, u32[]{:S(2)}) collective-permute-start(bf16[1024,256]{1,0:T(8,128)(2,1)S(1)} %pad_maximum_fusion.1), channel_id=1, source_target_pairs={{0,24},{4,28},{8,0},{12,4},{16,8},{20,12},{24,16},{28,20},{1,25},{... | collective-permute-start | bytes 1572872 | tf_op jit(solution)/shard_map/ppermute | solution.py:56
  120.7 26.0 %collective-permute-start.2 = (bf16[2048,256]{1,0:T(8,128)(2,1)}, bf16[2048,256]{1,0:T(8,128)(2,1)S(1)}, u32[]{:S(2)}, u32[]{:S(2)}) collective-permute-start(bf16[2048,256]{1,0:T(8,128)(2,1)} %pad_maximum_fusion), channel_id=1, source_target_pairs={{0,16},{4,20},{8,24},{12,28},{16,0},{20,4},{24,8},{28,12},{1,17},{... | collective-permute-start | bytes 3145736 | tf_op jit(solution)/shard_map/ppermute | solution.py:56
  124.5 161.3 %all-reduce.6.cloned.1.call-start = ((), (), s32[]{:S(2)}) async-start(), calls=%async_computation.3 | async-start | bytes 262144 | tf_op jit(solution)/shard_map/psum | solution.py:65
  147.8 8.2 %copy-start.4 = (bf16[32,8,8,128]{3,2,1,0:T(8,128)(2,1)S(1)}, bf16[32,8,8,128]{3,2,1,0:T(8,128)(2,1)}, u32[]{:S(2)}) copy-start(bf16[32,8,8,128]{3,2,1,0:T(8,128)(2,1)} %copy-done.3) | copy-start | bytes 1572868
  150.1 8.6 %copy-start.9 = (f32[512,256]{1,0:T(8,128)S(1)}, f32[512,256]{1,0:T(8,128)}, u32[]{:S(2)}) copy-start(f32[512,256]{1,0:T(8,128)} %reduce-scatter.2.cloned.1.call-done) | copy-start | bytes 1572868
  150.1 8.6 %copy-start.11 = (bf16[256,256]{1,0:T(8,128)(2,1)S(1)}, bf16[256,256]{1,0:T(8,128)(2,1)}, u32[]{:S(2)}) copy-start(bf16[256,256]{1,0:T(8,128)(2,1)} %param.16) | copy-start | bytes 393220
Sparse Core Ops, SparseCore 0:
  44.3 53.9 reduce-scatter.1
  124.6 124.4 all-reduce.3
  252.2 33.5 all-reduce.5
